TPU v7x, 32 devices: a whole 2x2x4 slice. The times are simulated.
32 devices in a mesh: dom: 8 (over z, x), grp: 4 (over y, core).
Axes of the slice: x: 2, y: 2, z: 4, core: 2. Of those that a mesh axis runs over, the one named last changes fastest.
Arguments:
- heads: int32 [262144], P(('dom', 'grp')), may hold values from 0 to 2047
- tails: int32 [262144], P(('dom', 'grp')), may hold values from 0 to 4095, as said below
- signs: int32 [2, 262144], P(None, ('dom', 'grp')), may hold values from 0 to 4095
- edge_weights: float32 [262144], P(('dom', 'grp')), may hold values from 0.25 to 4
- ground: float32 [16384], P(('dom', 'grp')), may hold values from 2 to 40
Outputs:
- solution: float32 [24, 16384], P(None, ('dom', 'grp'))
- residual: float32 [24, 16384], P(None, ('dom', 'grp'))
Inputs may be any that keep to these rules, and one draw needn't show every extreme that they name: `tails`: every second endpoint is a vertex of the graph.
All inputs are finite; a program needn't handle non-finite values.
Results may differ from a plain program's by a relative error of at most 0.0003.
Values sent between devices are 32-bit elements; how exact they have to be, the bound alone decides.
No kernel may reach another device: no remote copies, remote signals or barrier semaphores. Data moves between devices by JAX's collectives and lax.ppermute only.
A program may use at most 64 MiB of HBM per device.

v0:
```python
import functools

import jax
import jax.numpy as jnp
from jax import lax
from jax.experimental import pallas as pl
from jax.experimental.pallas import tpu as pltpu
from jax.sharding import PartitionSpec as P

K = 24
HALF = 12
LANES = 128
SUB = 8
BF = jnp.bfloat16
F32 = jnp.float32


def row_of(block, r, count):
    return jnp.broadcast_to(block[r : r + 1, :], (count, LANES))


def bits_of(n):
    return (n - 1).bit_length()


class Sizes:
    def __init__(self, edev, verts, group):
        self.edev, self.verts, self.group = edev, verts, group
        self.domain = verts * group
        self.reach = self.domain // 2
        self.extent = self.domain + 2 * self.reach
        self.rows = K // group
        self.section = edev // LANES
        self.ground_rows = verts // LANES
        self.payload = -(-(5 * self.section + self.ground_rows) // SUB) * SUB
        self.regs = edev * group // (SUB * LANES)
        self.parts = self.regs * SUB // LANES
        self.strip = self.domain // 8
        self.blocks = (self.strip // LANES, self.extent // 16 // LANES + 2)
        self.most = (2 * self.blocks[0], self.blocks[1])
        self.window = self.extent // 16 + 64
        self.further = self.extent // 64
        self.batch = 16

    def padded(self, which):
        return (self.domain, self.extent)[which] // LANES + self.most[which]

    def pack(self, heads, tails, signs):
        strip = heads // self.strip
        turned = jnp.where(strip % 2 == 1, self.extent - 1 - tails, tails)
        key = strip * self.extent + turned
        key = key * self.strip + heads % self.strip
        return (key << self.rows) | signs

    def unpack(self, key):
        key = jnp.right_shift(key, self.rows)
        low, key = key & (self.strip - 1), jnp.right_shift(key, bits_of(self.strip))
        turned, strip = key & (self.extent - 1), jnp.right_shift(key, bits_of(self.extent))
        tails = jnp.where(strip & 1 == 1, self.extent - 1 - turned, turned)
        return strip * self.strip + low, tails


def flip_mask(size, level):
    low = bits_of(size.regs)
    if level >= low + 10:
        return None
    if level < low + 3:
        place = lax.broadcasted_iota(jnp.int32, (SUB, LANES), 0)
        bit = level - low
    else:
        place = lax.broadcasted_iota(jnp.int32, (SUB, LANES), 1)
        bit = level - low - 3
    return -(jnp.right_shift(place, bit) & 1)


def partner(size, j):
    low = bits_of(size.regs)
    axis, bit = (0, j - low) if j < low + 3 else (1, j - low - 3)
    place = lax.broadcasted_iota(jnp.int32, (SUB, LANES), axis)
    lower = (jnp.right_shift(place, bit) & 1) == 0
    index = jnp.bitwise_xor(place, 1 << bit)
    return axis, index, lower


def sort_edges(size, keys, weights):
    low = bits_of(size.regs)
    levels = low + 10

    def between(group, stages):
        key = {v: keys[v] for v in group}
        weight = {v: weights[v] for v in group}
        for level, j in stages:
            for v in group:
                if v >> j & 1:
                    continue
                a, b = v, v | 1 << j
                if level < low and v >> level & 1:
                    a, b = b, a
                swap = key[a] > key[b]
                key[a], key[b] = jnp.where(swap, key[b], key[a]), jnp.where(swap, key[a], key[b])
                weight[a], weight[b] = (
                    jnp.where(swap, weight[b], weight[a]),
                    jnp.where(swap, weight[a], weight[b]),
                )
        for v in group:
            keys[v] = key[v]
            weights[v] = weight[v]

    def registers(level):
        top = min(level, low)
        if top > 3:
            for v in range(8):
                between(list(range(v, size.regs, 8)), [(level, j) for j in range(top - 1, 2, -1)])
        for v in range(0, size.regs, 8):
            between(list(range(v, v + 8)), [(level, j) for j in range(min(top, 3) - 1, -1, -1)])

    for v in range(0, size.regs, 8):
        between(list(range(v, v + 8)), [(level, j) for level in (1, 2, 3) for j in range(level - 1, -1, -1)])
    for level in range(4, low):
        registers(level)

    for level in range(low, levels + 1):
        before = flip_mask(size, level - 1) if level > low else None
        now = flip_mask(size, level)
        flip = now if before is None else before if now is None else jnp.bitwise_xor(before, now)
        stages = [partner(size, j) for j in range(level - 1, low - 1, -1)]

        wide = min(32, size.regs)

        def across(i, carry, flip=flip, stages=stages):
            group = [i * wide + u for u in range(wide)]
            key = [jnp.bitwise_xor(keys[v], flip) for v in group]
            weight = [weights[v] for v in group]
            for axis, index, lower in stages:
                for u in range(wide):
                    k, w = key[u], weight[u]
                    other = jnp.take_along_axis(k, index, axis=axis, mode="promise_in_bounds")
                    other_w = jnp.take_along_axis(w, index, axis=axis, mode="promise_in_bounds")
                    best = jnp.where(lower, jnp.minimum(k, other), jnp.maximum(k, other))
                    weight[u] = jnp.where(best == k, w, other_w)
                    key[u] = best
            for u, v in enumerate(group):
                keys[v] = key[u]
                weights[v] = weight[u]
            return carry

        lax.fori_loop(0, size.regs // wide, across, 0)
        registers(level)


def sort_kernel(size, place, pay, key_out, heads_out, tails_out, weight_out, bounds, keys, weights):
    word, shift = place[0], place[1]
    per = size.section // SUB
    mask = (1 << size.rows) - 1

    def section(which, g, c):
        return pay[g, which * size.section + c * SUB : which * size.section + (c + 1) * SUB, :]

    for g in range(size.group):
        for c in range(per):
            heads = section(0, g, c).astype(jnp.int32)
            tails = section(1, g, c).astype(jnp.int32)
            signs = jnp.where(word == 0, section(2, g, c), section(3, g, c)).astype(jnp.int32)
            v = g * per + c
            keys[v] = size.pack(heads, tails, jnp.right_shift(signs, shift) & mask)
            weights[v] = section(4, g, c)
    sort_edges(size, keys, weights)
    ends = [size.unpack(keys[v]) for v in range(size.regs)]
    lane = lax.broadcasted_iota(jnp.int32, (1, LANES), 1)
    far = rare = lane < 0
    for which in range(2):
        least = functools.reduce(jnp.minimum, [end[which] for end in ends])
        most = functools.reduce(jnp.maximum, [end[which] for end in ends])
        least = jnp.min(least, axis=0, keepdims=True)
        most = jnp.max(most, axis=0, keepdims=True)
        bounds[2 * which : 2 * which + 1, :] = least
        bounds[2 * which + 1 : 2 * which + 2, :] = most
        if which == 1:
            far = far | (most - (least & -8) >= size.window)
            rare = rare | (most - (least & -8) >= size.window + size.further)
        least, most = least // LANES, most // LANES
        far = far | (most - least >= size.blocks[which])
        rare = rare | (most - least >= size.most[which])
    runs = jnp.where(far, lane, LANES)
    count = jnp.sum(far.astype(F32), axis=1, keepdims=True)
    rare = jnp.max(jnp.where(rare, 1.0, 0.0), axis=1, keepdims=True)
    rare, count = rare.astype(jnp.int32), count.astype(jnp.int32)
    for step in (1, 2, 4, 8, 16, 32, 64):
        after = jnp.where(lane + step < LANES, jnp.roll(runs, -step, axis=1), LANES)
        runs = jnp.minimum(runs, after)
    bounds[4:5, :] = runs
    bounds[5:6, :] = jnp.broadcast_to(rare, (1, LANES))
    bounds[6:7, :] = jnp.broadcast_to(count, (1, LANES))
    for j in range(size.parts):
        here = range(j * 16, (j + 1) * 16)
        key = jnp.concatenate([keys[v] for v in here], axis=0).T
        key_out[j] = key
        heads_out[j], tails_out[j] = size.unpack(key)
        weight_out[j] = jnp.concatenate([weights[v] for v in here], axis=0).T


def halves_of(value):
    high = value.astype(BF).astype(F32)
    return jnp.concatenate([high, value - high], axis=0).astype(BF)


def row(ref, j, run, count):
    return jnp.broadcast_to(ref[j, pl.ds(run, 1), :], (count, LANES))


def next_far(bounds, run):
    following = bounds[4, jnp.minimum(run + 1, LANES - 1)]
    return jnp.where(run + 1 < LANES, following, LANES)


def one_hot(size, index, run, start, window):
    iota = lax.broadcasted_iota(jnp.int32, (16, LANES), 0)
    rows = [(iota + 16 * m).astype(F32).astype(BF) for m in range(16)]
    zero, one = jnp.zeros((16, LANES), BF), jnp.ones((16, LANES), BF)
    hot = []
    for j in range(size.parts):
        column = []
        for at in range(0, window, 256):
            local = (row(index, j, run, 16) - (start + at)).astype(F32).astype(BF)
            count = min(256, window - at) // 16
            column += [jnp.where(local == rows[m], one, zero) for m in range(count)]
        hot.append(jnp.concatenate(column, axis=0))
    return jnp.concatenate(hot, axis=1)


def times(left, right):
    return lax.dot_general(left, right, (((1,), (1,)), ((), ())), preferred_element_type=F32)


def add_blocks(size, heads, run, first, begin, end, pair, acc, valid=True):
    start = (first + begin) * LANES
    if valid is not True:
        start = jnp.where(valid, start, -(1 << 20))
    got = times(pair, one_hot(size, heads, run, start, (end - begin) * LANES))
    for b in range(end - begin):
        acc[first + begin + b] += got[:, b * LANES : (b + 1) * LANES]


def add_rows(size, tails, run, start, window, pair, acc, valid=True):
    start = pl.multiple_of(start, SUB)
    from_ = start if valid is True else jnp.where(valid, start, -(1 << 20))
    acc[pl.ds(start, window), 0:16] += times(one_hot(size, tails, run, from_, window), pair)


def first_block(bounds, which, run):
    return bounds[2 * which, run] // LANES


def last_block(bounds, which, run):
    return bounds[2 * which + 1, run] // LANES


def first_row(bounds, run):
    return bounds[2, run] & -8


def sweep(size, bounds, ends, make, make_far, accs, bufs):
    def fill(buf, base):
        for q in range(size.batch):
            for which, pair in enumerate(make(base + q)):
                buf[which, q] = pair

    heads, tails = ends
    acc_h, acc_t = accs

    def use(buf, base):
        for q in range(size.batch):
            run = base + q
            add_blocks(size, heads, run, first_block(bounds, 0, run), 0, size.blocks[0], buf[0, q], acc_h)
            add_rows(size, tails, run, first_row(bounds, run), size.window, buf[1, q], acc_t)

    fill(bufs[0], 0)

    def step(i, carry):
        base = i * 2 * size.batch
        use(bufs[0], base)
        fill(bufs[1], base + size.batch)
        use(bufs[1], base + size.batch)
        fill(bufs[0], (base + 2 * size.batch) % LANES)
        return carry

    lax.fori_loop(0, LANES // (2 * size.batch), step, 0)

    @pl.when(bounds[5, 0] == 0)
    def _():
        def four(i, run):
            for _ in range(4):
                valid, here = run < LANES, jnp.minimum(run, LANES - 1)
                full, beyond = make_far(here, False)
                first = first_block(bounds, 0, here)
                add_blocks(size, heads, here, first, size.blocks[0], size.most[0], full[0], acc_h, valid)
                start = first_row(bounds, here)
                add_rows(size, tails, here, start + size.window, size.further, full[1], acc_t, valid)
                if beyond is not None:
                    add_rows(size, tails, here, start, size.window, beyond[1], acc_t, valid)
                run = jnp.where(valid, next_far(bounds, here), LANES)
            return run

        lax.fori_loop(0, (bounds[6, 0] + 3) // 4, four, bounds[4, 0])

    @pl.when(bounds[5, 0] != 0)
    def _():
        def more(run):
            full, beyond = make_far(run, True)
            first, start = first_block(bounds, 0, run), first_row(bounds, run)

            def block(a, carry):
                add_blocks(size, heads, run, a, 0, 1, full[0], acc_h)
                return carry

            def window(m, carry):
                add_rows(size, tails, run, start + m * size.window, size.window, full[1], acc_t)
                return carry

            lax.fori_loop(first + size.blocks[0], last_block(bounds, 0, run) + 1, block, 0)
            lax.fori_loop(1, (bounds[3, run] - start) // size.window + 1, window, 0)
            if beyond is not None:
                add_blocks(size, heads, run, first, 0, size.blocks[0], beyond[0], acc_h)
                add_rows(size, tails, run, start, size.window, beyond[1], acc_t)
            return next_far(bounds, run)

        lax.while_loop(lambda run: run < LANES, more, bounds[4, 0])


def collect(size, acc_h, acc_t, out_l, out_r):
    shift = size.reach // LANES
    half = size.domain // LANES
    for a in range(size.extent // LANES):
        value = acc_t[a * LANES : (a + 1) * LANES, :].T
        value = value[0:8, :] + value[8:16, :]
        h = a - shift
        if 0 <= h < half:
            value += acc_h[h, 0:8] + acc_h[h, 8:16]
        out, at = (out_l, a) if a < half else (out_r, a - half)
        out[:, at * LANES : (at + 1) * LANES] = value


def clear(acc_h, acc_t):
    acc_h[...] = jnp.zeros_like(acc_h)
    acc_t[...] = jnp.zeros_like(acc_t)


def sketch_kernel(size, bounds, keys, heads, tails, weights, pay, out_l, out_r, acc_h, acc_t, buf_a, buf_b, tables):
    sub = lax.broadcasted_iota(jnp.int32, (SUB, LANES), 0)
    is_sign = sub < size.rows
    clear(acc_h, acc_t)

    def make(run):
        pairs = [[], []]
        for j in range(size.parts):
            weight = row(weights, j, run, SUB)
            bit = jnp.right_shift(row(keys, j, run, SUB), sub) & 1
            signed = (2 * bit - 1).astype(F32) * jnp.sqrt(weight)
            last = jnp.where(sub == size.rows, weight, 0.0)
            pairs[0].append(halves_of(jnp.where(is_sign, signed, last)))
            pairs[1].append(halves_of(jnp.where(is_sign, -signed, last)))
        return [jnp.concatenate(pair, axis=1) for pair in pairs]

    sweep(size, bounds, (heads, tails), make, lambda run, every: (make(run), None), (acc_h, acc_t), (buf_a, buf_b))
    collect(size, acc_h, acc_t, out_l, out_r)
    for g in range(size.group):
        for r in range(size.ground_rows):
            at = size.reach + g * size.verts + r * LANES
            out, at = (out_l, at) if at < size.domain else (out_r, at - size.domain)
            line = 5 * size.section + r
            value = jnp.broadcast_to(pay[g, line : line + 1, :], (SUB, LANES))
            out[:, at : at + LANES] += jnp.where(sub == size.rows, value, 0.0)


def operator_core(size, bounds, heads, tails, weights, table, out_l, out_r, bufs):
    acc_h, acc_t, buf_a, buf_b, tables = bufs
    clear(acc_h, acc_t)
    for a in range(size.extent // LANES):
        tables[a] = table[:, a * LANES : (a + 1) * LANES]
    ends = (heads, tails)

    def take(which, low, high, a, out):
        shift = size.reach // LANES if which == 0 else 0
        got = jnp.take_along_axis(tables[shift + a], low, axis=1, mode="promise_in_bounds")
        return jnp.where(high == a, got, out)

    nothing = jnp.zeros((SUB, LANES), F32)

    def gathered(run, blocks):
        pairs = [[], []]
        for j in range(size.parts):
            weight = row(weights, j, run, SUB)
            for which in range(2):
                index = row(ends[which], j, run, SUB)
                first, (begin, end) = first_block(bounds, which, run), blocks[which]
                low, high = index % LANES, index // LANES
                if end is None:
                    out = lax.fori_loop(
                        first + begin, last_block(bounds, which, run) + 1,
                        lambda a, out: take(which, low, high, a, out), nothing,
                    )
                else:
                    out = nothing
                    for a in range(begin, end):
                        out = take(which, low, high, first + a, out)
                pairs[1 - which].append(halves_of(out * weight))
        return [jnp.concatenate(pair, axis=1) for pair in pairs]

    def make(run):
        return gathered(run, [(0, size.blocks[which]) for which in range(2)])

    def make_far(run, every):
        ends_at = [None, None] if every else size.most
        return (
            gathered(run, [(0, ends_at[which]) for which in range(2)]),
            gathered(run, [(size.blocks[which], ends_at[which]) for which in range(2)]),
        )

    sweep(size, bounds, ends, make, make_far, (acc_h, acc_t), (buf_a, buf_b))
    collect(size, acc_h, acc_t, out_l, out_r)


def halves(size, own_l, own_r, got_l, got_r):
    return ((0, own_l, got_l), (size.domain, own_r, got_r))


def first_kernel(size, bounds, heads, tails, weights, own_l, own_r, got_l, got_r, out_l, out_r, v, diag, *bufs):
    sub = lax.broadcasted_iota(jnp.int32, (SUB, size.domain), 0)
    for at, own, got in halves(size, own_l, own_r, got_l, got_r):
        total = own[...] + got[...]
        spread = jnp.broadcast_to(total[size.rows : size.rows + 1, :], total.shape)
        safe = jnp.where(spread > 0.0, spread, 1.0)
        diag[:, at : at + size.domain] = safe
        v[:, at : at + size.domain] = jnp.where(sub < size.rows, total / safe, 0.0)
    operator_core(size, bounds, heads, tails, weights, v, out_l, out_r, bufs)


def next_v(size, own_l, own_r, got_l, got_r, diag, v):
    for at, own, got in halves(size, own_l, own_r, got_l, got_r):
        v[:, at : at + size.domain] = (own[...] + got[...]) / diag[:, at : at + size.domain]


def second_kernel(size, bounds, heads, tails, weights, own_l, own_r, got_l, got_r, diag, out_l, out_r, v, *bufs):
    next_v(size, own_l, own_r, got_l, got_r, diag, v)
    operator_core(size, bounds, heads, tails, weights, v, out_l, out_r, bufs)


def third_kernel(size, bounds, heads, tails, weights, own_l, own_r, got_l, got_r, diag, v0, v1, out_l, out_r, v2, moments, *bufs):
    next_v(size, own_l, own_r, got_l, got_r, diag, v2)
    operator_core(size, bounds, heads, tails, weights, v2, out_l, out_r, bufs)
    lane = lax.broadcasted_iota(jnp.int32, (SUB, LANES), 1)
    middle = slice(size.reach, size.reach + size.domain)
    weighted = diag[:, middle] * v0[:, middle]
    other = diag[:, middle] * v1[:, middle]
    sums = [
        weighted * v0[:, middle],
        weighted * v1[:, middle],
        other * v1[:, middle],
        other * v2[:, middle],
        diag[:, middle] * v2[:, middle] * v2[:, middle],
        v2[:, : size.domain] * out_l[...] + v2[:, size.domain :] * out_r[...],
    ]
    out = jnp.zeros((SUB, LANES), F32)
    for k, value in enumerate(sums):
        out = jnp.where(lane == k, jnp.sum(value, axis=1, keepdims=True), out)
    for d in range(moments.shape[0]):
        moments[d] = out


def coefficients(mu):
    zero = jnp.zeros_like(mu[0])

    def inner(a, b):
        total = None
        for i, x in enumerate(a):
            for j, y in enumerate(b):
                term = mu[i + j] if x is None and y is None else mu[i + j] * (y if x is None else x if y is None else x * y)
                total = term if total is None else total + term
        return total

    def image(a):
        a = [jnp.ones_like(zero) if x is None else x for x in a] + [zero]
        return [a[0]] + [a[i] - a[i - 1] for i in range(1, len(a))]

    def ratio(top, bottom):
        return jnp.where(bottom > 0.0, top / jnp.where(bottom > 0.0, bottom, 1.0), 0.0)

    rho, pi, x = [jnp.ones_like(zero)], [jnp.ones_like(zero)], []
    gamma = inner(rho, rho)
    for step in range(3):
        moved = image(pi)
        alpha = ratio(gamma, inner(pi, moved))
        x = [(x[i] if i < len(x) else zero) + alpha * pi[i] for i in range(len(pi))]
        rho = [(rho[i] if i < len(rho) else zero) - alpha * moved[i] for i in range(len(moved))]
        if step < 2:
            following = inner(rho, rho)
            beta = ratio(following, gamma)
            pi = [rho[i] + (beta * pi[i] if i < len(pi) else zero) for i in range(len(rho))]
            gamma = following
    return x, rho


def last_kernel(size, moments, own_l, own_r, got_l, got_r, diag, v0, v1, v2, out):
    total = moments[0]
    for d in range(1, moments.shape[0]):
        total = total + moments[d]
    mu = [jnp.broadcast_to(total[:, k : k + 1], (SUB, LANES)) for k in range(6)]
    x, rho = coefficients(mu)
    x = [value[:, :1] for value in x]
    rho = [value[:, :1] for value in rho]
    for g in range(size.group):
        at = size.reach + g * size.verts
        here = slice(at, at + size.verts)
        if at < size.domain:
            sums = own_l[:, here] + got_l[:, g * size.verts : (g + 1) * size.verts]
        else:
            back = at - size.domain
            inside = slice(back, back + size.verts)
            sums = own_r[:, inside] + got_r[:, inside]
        a, b, c, scale = v0[:, here], v1[:, here], v2[:, here], diag[:, here]
        out[g, 0] = x[0] * a + x[1] * b + x[2] * c
        out[g, 1] = scale * (rho[0] * a + rho[1] * b + rho[2] * c) + rho[3] * sums


def order_kernel(size, parts, x, r):
    for g in range(size.group):
        here = slice(g * size.rows, (g + 1) * size.rows)
        x[here, :] = parts[g, 0, : size.rows]
        r[here, :] = parts[g, 1, : size.rows]


def on_device(heads, tails, signs, edge_weights, ground):
    group = lax.axis_size("grp")
    count = lax.axis_size("dom")
    size = Sizes(heads.shape[0], ground.shape[0], group)
    vmem = pl.BlockSpec(memory_space=pltpu.VMEM)
    smem = pl.BlockSpec(memory_space=pltpu.SMEM)
    params = pltpu.CompilerParams(vmem_limit_bytes=48 * 1024 * 1024)

    def flat(value):
        return value.astype(F32).reshape(-1, LANES)

    parts = [flat(heads), flat(tails), flat(signs[0]), flat(signs[1]), flat(edge_weights), flat(ground)]
    used = sum(part.shape[0] for part in parts)
    parts.append(jnp.zeros((size.payload - used, LANES), F32))
    pay = lax.all_gather(jnp.concatenate(parts, axis=0), "grp")

    half = jax.ShapeDtypeStruct((SUB, size.domain), F32)
    full = jax.ShapeDtypeStruct((SUB, size.extent), F32)

    odd = lax.axis_index("dom") % 2 == 1

    def exchange(left, right):
        got = []
        for base in range(2):
            lower = [i for i in range(base, count - 1, 2)]
            pairs = [(i, i + 1) for i in lower] + [(i + 1, i) for i in lower]
            sent = jnp.where(odd, left, right) if base == 0 else jnp.where(odd, right, left)
            got.append(lax.ppermute(sent, "dom", pairs))
        return jnp.where(odd, got[0], got[1]), jnp.where(odd, got[1], got[0])

    me = lax.axis_index("grp")
    first_row = me * size.rows
    place = jnp.stack([first_row // HALF, first_row % HALF]).astype(jnp.int32)
    spread = (size.parts, LANES, LANES)
    keys, heads, tails, weights, bounds = pl.pallas_call(
        functools.partial(sort_kernel, size),
        out_shape=(
            jax.ShapeDtypeStruct(spread, jnp.int32),
            jax.ShapeDtypeStruct(spread, jnp.int32),
            jax.ShapeDtypeStruct(spread, jnp.int32),
            jax.ShapeDtypeStruct(spread, F32),
            jax.ShapeDtypeStruct((SUB, LANES), jnp.int32),
        ),
        in_specs=[smem, vmem],
        out_specs=(vmem,) * 5,
        scratch_shapes=[
            pltpu.VMEM((size.regs, SUB, LANES), jnp.int32),
            pltpu.VMEM((size.regs, SUB, LANES), F32),
        ],
        compiler_params=params,
        name="sort_edges",
    )(place, pay)
    edges = (bounds, heads, tails, weights)
    edge_specs = [smem, vmem, vmem, vmem]
    scratch = [
        pltpu.VMEM((size.padded(0), 16, LANES), F32),
        pltpu.VMEM((size.extent + size.window + size.further, LANES), F32),
        pltpu.VMEM((2, size.batch, 16, size.parts * LANES), BF),
        pltpu.VMEM((2, size.batch, 16, size.parts * LANES), BF),
        pltpu.VMEM((size.padded(1) + size.most[0], SUB, LANES), F32),
    ]
    acc = pl.pallas_call(
        functools.partial(sketch_kernel, size),
        out_shape=(half, half),
        in_specs=edge_specs + [vmem] * 2,
        out_specs=(vmem, vmem),
        scratch_shapes=scratch,
        compiler_params=params,
        name="sketch",
    )(bounds, keys, heads, tails, weights, pay)
    got = exchange(*acc)
    *acc, v0, diag = pl.pallas_call(
        functools.partial(first_kernel, size),
        out_shape=(half, half, full, full),
        in_specs=edge_specs + [vmem] * 4,
        out_specs=(vmem,) * 4,
        scratch_shapes=scratch,
        compiler_params=params,
        name="operator_first",
    )(*edges, *acc, *got)
    got = exchange(*acc)
    *acc, v1 = pl.pallas_call(
        functools.partial(second_kernel, size),
        out_shape=(half, half, full),
        in_specs=edge_specs + [vmem] * 5,
        out_specs=(vmem,) * 3,
        scratch_shapes=scratch,
        compiler_params=params,
        name="operator_second",
    )(*edges, *acc, *got, diag)
    got = exchange(*acc)
    *acc, v2, moments = pl.pallas_call(
        functools.partial(third_kernel, size),
        out_shape=(half, half, full, jax.ShapeDtypeStruct((count, SUB, LANES), F32)),
        in_specs=edge_specs + [vmem] * 7,
        out_specs=(vmem,) * 4,
        scratch_shapes=scratch,
        compiler_params=params,
        name="operator_third",
    )(*edges, *acc, *got, diag, v0, v1)
    got_l, got_r = exchange(acc[0][:, : size.reach], acc[1][:, size.reach :])
    shared = lax.all_to_all(moments, "dom", 0, 0)
    out = pl.pallas_call(
        functools.partial(last_kernel, size),
        out_shape=jax.ShapeDtypeStruct((group, 2, SUB, size.verts), F32),
        in_specs=[vmem] * 9,
        out_specs=vmem,
        compiler_params=params,
        name="combine",
    )(shared, *acc, got_l, got_r, diag, v0, v1, v2)
    out = lax.all_to_all(out, "grp", 0, 0)
    result = jax.ShapeDtypeStruct((K, size.verts), F32)
    return pl.pallas_call(
        functools.partial(order_kernel, size),
        out_shape=(result, result),
        in_specs=[vmem],
        out_specs=(vmem, vmem),
        compiler_params=params,
        name="order",
    )(out)


def solution(mesh):
    in_specs = (
        P(("dom", "grp")),
        P(("dom", "grp")),
        P(None, ("dom", "grp")),
        P(("dom", "grp")),
        P(("dom", "grp")),
    )
    out_specs = (P(None, ("dom", "grp")), P(None, ("dom", "grp")))
    return jax.shard_map(
        on_device, mesh=mesh, in_specs=in_specs, out_specs=out_specs, check_vma=False
    )
```

profile of v0, /device:TPU:0, one launch (start us, length us, event | category | flops | bytes accessed | tf_op | source)
XLA Modules:
  0.0 110.3 jit_solution(13082089277350580484)
XLA Ops:
  0.7 0.0 copy-start
  0.7 0.0 copy-start.1
  0.7 1.0 slice_convert_fusion
  1.7 0.0 copy-done
  1.7 0.0 copy-done.1
  1.7 0.0 copy-start.2
  1.7 0.0 copy-start.3
  1.7 0.7 copy-done.2
  2.4 0.0 copy-done.3
  2.5 9.4 %all-gather = f32[1312,128]{1,0:T(8,128)S(1)} all-gather(f32[328,128]{1,0:T(8,128)S(1)} %concatenate.3), channel_id=2, replica_groups=mesh['dom'=8,'grp'=4] {'grp'}, dimensions={0}, use_global_device_ids=true | all-gather | bytes 839680 | tf_op jit(solution)/shard_map/all_gather | solution.py:546
  11.9 0.1 pad_add_fusion.place
  12.0 5.5 %sort_edges.1 = (s32[2,128,128]{2,1,0:T(8,128)S(1)}, s32[2,128,128]{2,1,0:T(8,128)S(1)}, s32[2,128,128]{2,1,0:T(8,128)S(1)}, f32[2,128,128]{2,1,0:T(8,128)S(1)}, s32[8,128]{1,0:T(8,128)S(1)}) custom-call(s32[2]{0:T(128)S(1)} %pad_add_fusion.place, f32[4,328,128]{2,1,0:T(8,128)S(1)} %bitcast.11), custom_call_target="tpu_custom_call" | custom-call | tf_op jit(solution)/shard_map/sort_edges/pallas_call | solution.py:566
  17.5 8.8 %sketch.1 = (f32[8,2048]{1,0:T(8,128)S(1)}, f32[8,2048]{1,0:T(8,128)S(1)}) custom-call(s32[8,128]{1,0:T(8,128)S(1)} %get-tuple-element.20.bounds, s32[2,128,128]{2,1,0:T(8,128)S(1)} %get-tuple-element.24.keys, s32[2,128,128]{2,1,0:T(8,128)S(1)} %get-tuple-element.21.heads, s32[2,128,128]{2,1,0:T(8,128)S(1)} %get-tuple-element.22.tails, ...), custom_call_target="tpu_custom_call" | custom-call | tf_op jit(solution)/shard_map/sketch/pallas_call | solution.py:593
  26.4 0.7 collective-permute-start.1
  27.1 4.3 %collective-permute-start = (f32[8,2048]{1,0:T(8,128)S(1)}, f32[8,2048]{1,0:T(8,128)S(1)}, u32[]{:S(2)}, u32[]{:S(2)}) collective-permute-start(f32[8,2048]{1,0:T(8,128)S(1)} %get-tuple-element.51), channel_id=1, source_target_pairs={{0,4},{8,12},{16,20},{24,28},{4,0},{12,8},{20,16},{28,24},{1,5},{9... | collective-permute-start | bytes 196616 | tf_op jit(solution)/shard_map/ppermute | solution.py:559
  31.4 0.0 collective-permute-done.1
  31.4 2.6 %collective-permute-done = f32[8,2048]{1,0:T(8,128)S(1)} collective-permute-done((f32[8,2048]{1,0:T(8,128)S(1)}, f32[8,2048]{1,0:T(8,128)S(1)}, u32[]{:S(2)}, u32[]{:S(2)}) %collective-permute-start) | collective-permute-done | bytes 65568 | tf_op jit(solution)/shard_map/ppermute | solution.py:559
  34.0 11.5 %operator_first.1 = (f32[8,2048]{1,0:T(8,128)S(1)}, f32[8,2048]{1,0:T(8,128)S(1)}, f32[8,4096]{1,0:T(8,128)S(1)}, f32[8,4096]{1,0:T(8,128)S(1)}) custom-call(s32[8,128]{1,0:T(8,128)S(1)} %get-tuple-element.20.bounds, s32[2,128,128]{2,1,0:T(8,128)S(1)} %get-tuple-element.21.heads, s32[2,128,128]{2,1,0:T(8,128)S(1)} %get-tuple-element.22.tails, ...), custom_call_target="tpu_custom_call" | custom-call | tf_op jit(solution)/shard_map/operator_first/pallas_call | solution.py:603
  45.6 0.7 collective-permute-start.3
  46.3 5.3 %collective-permute-start.2 = (f32[8,2048]{1,0:T(8,128)S(1)}, f32[8,2048]{1,0:T(8,128)S(1)}, u32[]{:S(2)}, u32[]{:S(2)}) collective-permute-start(f32[8,2048]{1,0:T(8,128)S(1)} %get-tuple-element.47), channel_id=1, source_target_pairs={{0,4},{8,12},{16,20},{24,28},{4,0},{12,8},{20,16},{28,24},{1,5},{9... | collective-permute-start | bytes 196616 | tf_op jit(solution)/shard_map/ppermute | solution.py:559
  51.5 0.0 collective-permute-done.3
  51.5 2.3 %collective-permute-done.2 = f32[8,2048]{1,0:T(8,128)S(1)} collective-permute-done((f32[8,2048]{1,0:T(8,128)S(1)}, f32[8,2048]{1,0:T(8,128)S(1)}, u32[]{:S(2)}, u32[]{:S(2)}) %collective-permute-start.2) | collective-permute-done | bytes 65568 | tf_op jit(solution)/shard_map/ppermute | solution.py:559
  53.8 11.3 %operator_second.1 = (f32[8,2048]{1,0:T(8,128)S(1)}, f32[8,2048]{1,0:T(8,128)S(1)}, f32[8,4096]{1,0:T(8,128)S(1)}) custom-call(s32[8,128]{1,0:T(8,128)S(1)} %get-tuple-element.20.bounds, s32[2,128,128]{2,1,0:T(8,128)S(1)} %get-tuple-element.21.heads, s32[2,128,128]{2,1,0:T(8,128)S(1)} %get-tuple-element.22.tails, ...), custom_call_target="tpu_custom_call" | custom-call | tf_op jit(solution)/shard_map/operator_second/pallas_call | solution.py:613
  65.1 0.7 collective-permute-start.5
  65.8 5.3 %collective-permute-start.4 = (f32[8,2048]{1,0:T(8,128)S(1)}, f32[8,2048]{1,0:T(8,128)S(1)}, u32[]{:S(2)}, u32[]{:S(2)}) collective-permute-start(f32[8,2048]{1,0:T(8,128)S(1)} %get-tuple-element.43), channel_id=1, source_target_pairs={{0,4},{8,12},{16,20},{24,28},{4,0},{12,8},{20,16},{28,24},{1,5},{9... | collective-permute-start | bytes 196616 | tf_op jit(solution)/shard_map/ppermute | solution.py:559
  71.1 0.0 collective-permute-done.5
  71.1 2.2 %collective-permute-done.4 = f32[8,2048]{1,0:T(8,128)S(1)} collective-permute-done((f32[8,2048]{1,0:T(8,128)S(1)}, f32[8,2048]{1,0:T(8,128)S(1)}, u32[]{:S(2)}, u32[]{:S(2)}) %collective-permute-start.4) | collective-permute-done | bytes 65568 | tf_op jit(solution)/shard_map/ppermute | solution.py:559
  73.3 12.0 %operator_third.1 = (f32[8,2048]{1,0:T(8,128)S(1)}, f32[8,2048]{1,0:T(8,128)S(1)}, f32[8,4096]{1,0:T(8,128)S(1)}, f32[8,8,128]{2,1,0:T(8,128)}) custom-call(s32[8,128]{1,0:T(8,128)S(1)} %get-tuple-element.20.bounds, s32[2,128,128]{2,1,0:T(8,128)S(1)} %get-tuple-element.21.heads, s32[2,128,128]{2,1,0:T(8,128)S(1)} %get-tuple-element.22.tails, ...), custom_call_target="tpu_custom_call" | custom-call | tf_op jit(solution)/shard_map/operator_third/pallas_call | solution.py:623
  85.4 0.7 collective-permute-start.7
  86.0 5.1 %collective-permute-start.6 = (f32[8,1024]{1,0:T(8,128)S(1)}, f32[8,1024]{1,0:T(8,128)S(1)}, u32[]{:S(2)}, u32[]{:S(2)}) collective-permute-start(f32[8,1024]{1,0:T(8,128)S(1)} %get-tuple-element.39), channel_id=1, source_target_pairs={{0,4},{8,12},{16,20},{24,28},{4,0},{12,8},{20,16},{28,24},{1,5},{9... | collective-permute-start | bytes 98312 | tf_op jit(solution)/shard_map/ppermute | solution.py:559
  91.1 4.6 %all-to-all-start = ((f32[8,8,128]{2,1,0:T(8,128)}), f32[8,8,128]{2,1,0:T(8,128)S(1)}, u32[]{:S(2)}, u32[]{:S(2)}) async-start(f32[8,8,128]{2,1,0:T(8,128)} %get-tuple-element.34), calls=%async_computation | async-start | bytes 65536 | tf_op jit(solution)/shard_map/all_to_all | solution.py:633
  95.7 0.0 collective-permute-done.7
  95.7 0.0 collective-permute-done.6
  95.8 6.7 %all-to-all-done.moments = f32[8,8,128]{2,1,0:T(8,128)S(1)} async-done(((f32[8,8,128]{2,1,0:T(8,128)}), f32[8,8,128]{2,1,0:T(8,128)S(1)}, u32[]{:S(2)}, u32[]{:S(2)}) %all-to-all-start) | async-done | bytes 32800 | tf_op jit(solution)/shard_map/all_to_all | solution.py:633
  102.4 0.2 combine.1
  102.6 7.0 %all_to_all.10.parts = f32[4,2,8,512]{3,2,1,0:T(8,128)S(1)} all-to-all(f32[4,2,8,512]{3,2,1,0:T(8,128)S(1)} %combine.1), channel_id=1, replica_groups=mesh['dom'=8,'grp'=4] {'grp'}, dimensions={0} | all-to-all | bytes 262144 | tf_op jit(solution)/shard_map/all_to_all | solution.py:642
  109.6 0.7 order.1
  (11 shorter events, 0.2 us)
Async XLA Ops:
  0.7 1.0 copy-start
  0.7 1.0 copy-start.1
  1.7 0.8 copy-start.2
  1.7 0.7 copy-start.3
  26.4 5.0 %collective-permute-start.1 = (f32[8,2048]{1,0:T(8,128)S(1)}, f32[8,2048]{1,0:T(8,128)S(1)}, u32[]{:S(2)}, u32[]{:S(2)}) collective-permute-start(f32[8,2048]{1,0:T(8,128)S(1)} %get-tuple-element.50), channel_id=1, source_target_pairs={{4,8},{12,16},{20,24},{8,4},{16,12},{24,20},{5,9},{13,17},{21,25},... | collective-permute-start | bytes 196616 | tf_op jit(solution)/shard_map/ppermute | solution.py:559
  27.1 6.9 %collective-permute-start = (f32[8,2048]{1,0:T(8,128)S(1)}, f32[8,2048]{1,0:T(8,128)S(1)}, u32[]{:S(2)}, u32[]{:S(2)}) collective-permute-start(f32[8,2048]{1,0:T(8,128)S(1)} %get-tuple-element.51), channel_id=1, source_target_pairs={{0,4},{8,12},{16,20},{24,28},{4,0},{12,8},{20,16},{28,24},{1,5},{9... | collective-permute-start | bytes 196616 | tf_op jit(solution)/shard_map/ppermute | solution.py:559
  45.6 5.9 %collective-permute-start.3 = (f32[8,2048]{1,0:T(8,128)S(1)}, f32[8,2048]{1,0:T(8,128)S(1)}, u32[]{:S(2)}, u32[]{:S(2)}) collective-permute-start(f32[8,2048]{1,0:T(8,128)S(1)} %get-tuple-element.46), channel_id=1, source_target_pairs={{4,8},{12,16},{20,24},{8,4},{16,12},{24,20},{5,9},{13,17},{21,25},... | collective-permute-start | bytes 196616 | tf_op jit(solution)/shard_map/ppermute | solution.py:559
  46.3 7.5 %collective-permute-start.2 = (f32[8,2048]{1,0:T(8,128)S(1)}, f32[8,2048]{1,0:T(8,128)S(1)}, u32[]{:S(2)}, u32[]{:S(2)}) collective-permute-start(f32[8,2048]{1,0:T(8,128)S(1)} %get-tuple-element.47), channel_id=1, source_target_pairs={{0,4},{8,12},{16,20},{24,28},{4,0},{12,8},{20,16},{28,24},{1,5},{9... | collective-permute-start | bytes 196616 | tf_op jit(solution)/shard_map/ppermute | solution.py:559
  65.1 6.0 %collective-permute-start.5 = (f32[8,2048]{1,0:T(8,128)S(1)}, f32[8,2048]{1,0:T(8,128)S(1)}, u32[]{:S(2)}, u32[]{:S(2)}) collective-permute-start(f32[8,2048]{1,0:T(8,128)S(1)} %get-tuple-element.42), channel_id=1, source_target_pairs={{4,8},{12,16},{20,24},{8,4},{16,12},{24,20},{5,9},{13,17},{21,25},... | collective-permute-start | bytes 196616 | tf_op jit(solution)/shard_map/ppermute | solution.py:559
  65.8 7.5 %collective-permute-start.4 = (f32[8,2048]{1,0:T(8,128)S(1)}, f32[8,2048]{1,0:T(8,128)S(1)}, u32[]{:S(2)}, u32[]{:S(2)}) collective-permute-start(f32[8,2048]{1,0:T(8,128)S(1)} %get-tuple-element.43), channel_id=1, source_target_pairs={{0,4},{8,12},{16,20},{24,28},{4,0},{12,8},{20,16},{28,24},{1,5},{9... | collective-permute-start | bytes 196616 | tf_op jit(solution)/shard_map/ppermute | solution.py:559
  85.4 10.4 %collective-permute-start.7 = (f32[8,1024]{1,0:T(8,128)S(1)}, f32[8,1024]{1,0:T(8,128)S(1)}, u32[]{:S(2)}, u32[]{:S(2)}) collective-permute-start(f32[8,1024]{1,0:T(8,128)S(1)} %get-tuple-element.38), channel_id=1, source_target_pairs={{4,8},{12,16},{20,24},{8,4},{16,12},{24,20},{5,9},{13,17},{21,25},... | collective-permute-start | bytes 98312 | tf_op jit(solution)/shard_map/ppermute | solution.py:559
  86.0 9.7 %collective-permute-start.6 = (f32[8,1024]{1,0:T(8,128)S(1)}, f32[8,1024]{1,0:T(8,128)S(1)}, u32[]{:S(2)}, u32[]{:S(2)}) collective-permute-start(f32[8,1024]{1,0:T(8,128)S(1)} %get-tuple-element.39), channel_id=1, source_target_pairs={{0,4},{8,12},{16,20},{24,28},{4,0},{12,8},{20,16},{28,24},{1,5},{9... | collective-permute-start | bytes 98312 | tf_op jit(solution)/shard_map/ppermute | solution.py:559
  91.1 11.3 %all-to-all-start = ((f32[8,8,128]{2,1,0:T(8,128)}), f32[8,8,128]{2,1,0:T(8,128)S(1)}, u32[]{:S(2)}, u32[]{:S(2)}) async-start(f32[8,8,128]{2,1,0:T(8,128)} %get-tuple-element.34), calls=%async_computation | async-start | bytes 65536 | tf_op jit(solution)/shard_map/all_to_all | solution.py:633
where the time goes:
time: 111 us; the launch traced here: 110 us
  Pallas kernels  50.1 us (45%)
  starting transfers between devices  27.2 us (25%)
  blocking collectives  16.5 us (15%)
  waiting for transfers between devices  13.8 us (12%)
  other arithmetic  1.17 us (1%)
    ppermute x8, starting transfers between devices, exchange(): got.append(lax.ppermute(sent, 'dom', pairs))  22.6 us
    pallas_call x1, Pallas kernels, on_device(): pl.pallas_call(functools.partial(third_kernel, size), out_shape=(half, ha...  12 us
    pallas_call x1, Pallas kernels, on_device(): pl.pallas_call(functools.partial(first_kernel, size), out_shape=(half, ha...  11.5 us
    pallas_call x1, Pallas kernels, on_device(): pl.pallas_call(functools.partial(second_kernel, size), out_shape=(half, h...  11.3 us
    all_gather x1, blocking collectives, on_device(): pay = lax.all_gather(jnp.concatenate(parts, axis=0), 'grp')  9.44 us
    pallas_call x1, Pallas kernels, on_device(): pl.pallas_call(functools.partial(sketch_kernel, size), out_shape=(half, h...  8.84 us
    ppermute x8, waiting for transfers between devices, exchange(): got.append(lax.ppermute(sent, 'dom', pairs))  7.1 us
    all_to_all x1, blocking collectives, on_device(): out = lax.all_to_all(out, 'grp', 0, 0)  7.02 us
  transfers between devices with their start and end apart: 9, of which 4 were waited for; matrix products, arithmetic and copies ran while one was open for 0% of the time, Pallas kernels for 0%

commit v1 on v0

--- a/solution.py
+++ b/solution.py
@@ -38,8 +38,8 @@
         self.strip = self.domain // 8
         self.blocks = (self.strip // LANES, self.extent // 16 // LANES + 2)
         self.most = (2 * self.blocks[0], self.blocks[1])
-        self.window = self.extent // 16 + 64
-        self.further = self.extent // 64
+        self.window = self.extent // 16 + 32
+        self.further = self.extent // 64 + 32
         self.batch = 16
 
     def padded(self, which):

time: 111 us -> 112 us (level)
  starting transfers between devices: 27.2 us -> 29.9 us
  Pallas kernels: 50.1 us -> 48.3 us
    ppermute x8, starting transfers between devices: 22.6 us -> 24.9 us  [exchange(): got.append(lax.ppermute(sent, 'dom', pairs))]
where the time goes in v1:
time: 112 us
  Pallas kernels  48.3 us (43%)
  starting transfers between devices  29.9 us (27%)
  blocking collectives  16.5 us (15%)
  waiting for transfers between devices  14.6 us (13%)
  other arithmetic  1.17 us (1%)
    ppermute x8, starting transfers between devices, exchange(): got.append(lax.ppermute(sent, 'dom', pairs))  24.9 us
    pallas_call x1, Pallas kernels, on_device(): pl.pallas_call(functools.partial(third_kernel, size), out_shape=(half, ha...  11.7 us
    pallas_call x1, Pallas kernels, on_device(): pl.pallas_call(functools.partial(second_kernel, size), out_shape=(half, h...  11 us
    pallas_call x1, Pallas kernels, on_device(): pl.pallas_call(functools.partial(first_kernel, size), out_shape=(half, ha...  11 us
    all_gather x1, blocking collectives, on_device(): pay = lax.all_gather(jnp.concatenate(parts, axis=0), 'grp')  9.44 us
    pallas_call x1, Pallas kernels, on_device(): pl.pallas_call(functools.partial(sketch_kernel, size), out_shape=(half, h...  8.22 us
    ppermute x8, waiting for transfers between devices, exchange(): got.append(lax.ppermute(sent, 'dom', pairs))  7.99 us
    all_to_all x1, blocking collectives, on_device(): out = lax.all_to_all(out, 'grp', 0, 0)  7.02 us
  transfers between devices with their start and end apart: 9, of which 4 were waited for; matrix products, arithmetic and copies ran while one was open for 0% of the time, Pallas kernels for 0%

profile of v1, /device:TPU:0, one launch (start us, length us, event | category | flops | bytes accessed | tf_op | source)
XLA Modules:
  0.0 112.1 jit_solution(16279627345503502133)
XLA Ops:
  0.7 0.0 copy-start
  0.7 0.0 copy-start.1
  0.7 1.0 slice_convert_fusion
  1.7 0.0 copy-done
  1.7 0.0 copy-done.1
  1.7 0.0 copy-start.2
  1.7 0.0 copy-start.3
  1.7 0.7 copy-done.2
  2.4 0.0 copy-done.3
  2.5 9.4 %all-gather = f32[1312,128]{1,0:T(8,128)S(1)} all-gather(f32[328,128]{1,0:T(8,128)S(1)} %concatenate.3), channel_id=2, replica_groups=mesh['dom'=8,'grp'=4] {'grp'}, dimensions={0}, use_global_device_ids=true | all-gather | bytes 839680 | tf_op jit(solution)/shard_map/all_gather | solution.py:546
  11.9 0.1 pad_add_fusion.place
  12.0 5.5 %sort_edges.1 = (s32[2,128,128]{2,1,0:T(8,128)S(1)}, s32[2,128,128]{2,1,0:T(8,128)S(1)}, s32[2,128,128]{2,1,0:T(8,128)S(1)}, f32[2,128,128]{2,1,0:T(8,128)S(1)}, s32[8,128]{1,0:T(8,128)S(1)}) custom-call(s32[2]{0:T(128)S(1)} %pad_add_fusion.place, f32[4,328,128]{2,1,0:T(8,128)S(1)} %bitcast.11), custom_call_target="tpu_custom_call" | custom-call | tf_op jit(solution)/shard_map/sort_edges/pallas_call | solution.py:566
  17.5 8.2 %sketch.1 = (f32[8,2048]{1,0:T(8,128)S(1)}, f32[8,2048]{1,0:T(8,128)S(1)}) custom-call(s32[8,128]{1,0:T(8,128)S(1)} %get-tuple-element.20.bounds, s32[2,128,128]{2,1,0:T(8,128)S(1)} %get-tuple-element.24.keys, s32[2,128,128]{2,1,0:T(8,128)S(1)} %get-tuple-element.21.heads, s32[2,128,128]{2,1,0:T(8,128)S(1)} %get-tuple-element.22.tails, ...), custom_call_target="tpu_custom_call" | custom-call | tf_op jit(solution)/shard_map/sketch/pallas_call | solution.py:593
  25.8 0.7 collective-permute-start.1
  26.5 4.7 %collective-permute-start = (f32[8,2048]{1,0:T(8,128)S(1)}, f32[8,2048]{1,0:T(8,128)S(1)}, u32[]{:S(2)}, u32[]{:S(2)}) collective-permute-start(f32[8,2048]{1,0:T(8,128)S(1)} %get-tuple-element.51), channel_id=1, source_target_pairs={{0,4},{8,12},{16,20},{24,28},{4,0},{12,8},{20,16},{28,24},{1,5},{9... | collective-permute-start | bytes 196616 | tf_op jit(solution)/shard_map/ppermute | solution.py:559
  31.2 0.0 collective-permute-done.1
  31.2 3.0 %collective-permute-done = f32[8,2048]{1,0:T(8,128)S(1)} collective-permute-done((f32[8,2048]{1,0:T(8,128)S(1)}, f32[8,2048]{1,0:T(8,128)S(1)}, u32[]{:S(2)}, u32[]{:S(2)}) %collective-permute-start) | collective-permute-done | bytes 65568 | tf_op jit(solution)/shard_map/ppermute | solution.py:559
  34.2 11.0 %operator_first.1 = (f32[8,2048]{1,0:T(8,128)S(1)}, f32[8,2048]{1,0:T(8,128)S(1)}, f32[8,4096]{1,0:T(8,128)S(1)}, f32[8,4096]{1,0:T(8,128)S(1)}) custom-call(s32[8,128]{1,0:T(8,128)S(1)} %get-tuple-element.20.bounds, s32[2,128,128]{2,1,0:T(8,128)S(1)} %get-tuple-element.21.heads, s32[2,128,128]{2,1,0:T(8,128)S(1)} %get-tuple-element.22.tails, ...), custom_call_target="tpu_custom_call" | custom-call | tf_op jit(solution)/shard_map/operator_first/pallas_call | solution.py:603
  45.2 0.8 collective-permute-start.3
  46.1 5.4 %collective-permute-start.2 = (f32[8,2048]{1,0:T(8,128)S(1)}, f32[8,2048]{1,0:T(8,128)S(1)}, u32[]{:S(2)}, u32[]{:S(2)}) collective-permute-start(f32[8,2048]{1,0:T(8,128)S(1)} %get-tuple-element.47), channel_id=1, source_target_pairs={{0,4},{8,12},{16,20},{24,28},{4,0},{12,8},{20,16},{28,24},{1,5},{9... | collective-permute-start | bytes 196616 | tf_op jit(solution)/shard_map/ppermute | solution.py:559
  51.5 0.0 collective-permute-done.3
  51.5 2.7 %collective-permute-done.2 = f32[8,2048]{1,0:T(8,128)S(1)} collective-permute-done((f32[8,2048]{1,0:T(8,128)S(1)}, f32[8,2048]{1,0:T(8,128)S(1)}, u32[]{:S(2)}, u32[]{:S(2)}) %collective-permute-start.2) | collective-permute-done | bytes 65568 | tf_op jit(solution)/shard_map/ppermute | solution.py:559
  54.2 11.0 %operator_second.1 = (f32[8,2048]{1,0:T(8,128)S(1)}, f32[8,2048]{1,0:T(8,128)S(1)}, f32[8,4096]{1,0:T(8,128)S(1)}) custom-call(s32[8,128]{1,0:T(8,128)S(1)} %get-tuple-element.20.bounds, s32[2,128,128]{2,1,0:T(8,128)S(1)} %get-tuple-element.21.heads, s32[2,128,128]{2,1,0:T(8,128)S(1)} %get-tuple-element.22.tails, ...), custom_call_target="tpu_custom_call" | custom-call | tf_op jit(solution)/shard_map/operator_second/pallas_call | solution.py:613
  65.2 0.7 collective-permute-start.5
  65.9 6.2 %collective-permute-start.4 = (f32[8,2048]{1,0:T(8,128)S(1)}, f32[8,2048]{1,0:T(8,128)S(1)}, u32[]{:S(2)}, u32[]{:S(2)}) collective-permute-start(f32[8,2048]{1,0:T(8,128)S(1)} %get-tuple-element.43), channel_id=1, source_target_pairs={{0,4},{8,12},{16,20},{24,28},{4,0},{12,8},{20,16},{28,24},{1,5},{9... | collective-permute-start | bytes 196616 | tf_op jit(solution)/shard_map/ppermute | solution.py:559
  72.0 0.0 collective-permute-done.5
  72.1 2.3 %collective-permute-done.4 = f32[8,2048]{1,0:T(8,128)S(1)} collective-permute-done((f32[8,2048]{1,0:T(8,128)S(1)}, f32[8,2048]{1,0:T(8,128)S(1)}, u32[]{:S(2)}, u32[]{:S(2)}) %collective-permute-start.4) | collective-permute-done | bytes 65568 | tf_op jit(solution)/shard_map/ppermute | solution.py:559
  74.4 11.7 %operator_third.1 = (f32[8,2048]{1,0:T(8,128)S(1)}, f32[8,2048]{1,0:T(8,128)S(1)}, f32[8,4096]{1,0:T(8,128)S(1)}, f32[8,8,128]{2,1,0:T(8,128)}) custom-call(s32[8,128]{1,0:T(8,128)S(1)} %get-tuple-element.20.bounds, s32[2,128,128]{2,1,0:T(8,128)S(1)} %get-tuple-element.21.heads, s32[2,128,128]{2,1,0:T(8,128)S(1)} %get-tuple-element.22.tails, ...), custom_call_target="tpu_custom_call" | custom-call | tf_op jit(solution)/shard_map/operator_third/pallas_call | solution.py:623
  86.1 0.7 collective-permute-start.7
  86.8 5.7 %collective-permute-start.6 = (f32[8,1024]{1,0:T(8,128)S(1)}, f32[8,1024]{1,0:T(8,128)S(1)}, u32[]{:S(2)}, u32[]{:S(2)}) collective-permute-start(f32[8,1024]{1,0:T(8,128)S(1)} %get-tuple-element.39), channel_id=1, source_target_pairs={{0,4},{8,12},{16,20},{24,28},{4,0},{12,8},{20,16},{28,24},{1,5},{9... | collective-permute-start | bytes 98312 | tf_op jit(solution)/shard_map/ppermute | solution.py:559
  92.5 5.0 %all-to-all-start = ((f32[8,8,128]{2,1,0:T(8,128)}), f32[8,8,128]{2,1,0:T(8,128)S(1)}, u32[]{:S(2)}, u32[]{:S(2)}) async-start(f32[8,8,128]{2,1,0:T(8,128)} %get-tuple-element.34), calls=%async_computation | async-start | bytes 65536 | tf_op jit(solution)/shard_map/all_to_all | solution.py:633
  97.6 0.0 collective-permute-done.7
  97.6 0.0 collective-permute-done.6
  97.6 6.7 %all-to-all-done.moments = f32[8,8,128]{2,1,0:T(8,128)S(1)} async-done(((f32[8,8,128]{2,1,0:T(8,128)}), f32[8,8,128]{2,1,0:T(8,128)S(1)}, u32[]{:S(2)}, u32[]{:S(2)}) %all-to-all-start) | async-done | bytes 32800 | tf_op jit(solution)/shard_map/all_to_all | solution.py:633
  104.2 0.2 combine.1
  104.4 7.0 %all_to_all.10.parts = f32[4,2,8,512]{3,2,1,0:T(8,128)S(1)} all-to-all(f32[4,2,8,512]{3,2,1,0:T(8,128)S(1)} %combine.1), channel_id=1, replica_groups=mesh['dom'=8,'grp'=4] {'grp'}, dimensions={0} | all-to-all | bytes 262144 | tf_op jit(solution)/shard_map/all_to_all | solution.py:642
  111.5 0.7 order.1
  (11 shorter events, 0.2 us)
Async XLA Ops:
  0.7 1.0 copy-start
  0.7 1.0 copy-start.1
  1.7 0.8 copy-start.2
  1.7 0.7 copy-start.3
  25.8 5.4 %collective-permute-start.1 = (f32[8,2048]{1,0:T(8,128)S(1)}, f32[8,2048]{1,0:T(8,128)S(1)}, u32[]{:S(2)}, u32[]{:S(2)}) collective-permute-start(f32[8,2048]{1,0:T(8,128)S(1)} %get-tuple-element.50), channel_id=1, source_target_pairs={{4,8},{12,16},{20,24},{8,4},{16,12},{24,20},{5,9},{13,17},{21,25},... | collective-permute-start | bytes 196616 | tf_op jit(solution)/shard_map/ppermute | solution.py:559
  26.5 7.7 %collective-permute-start = (f32[8,2048]{1,0:T(8,128)S(1)}, f32[8,2048]{1,0:T(8,128)S(1)}, u32[]{:S(2)}, u32[]{:S(2)}) collective-permute-start(f32[8,2048]{1,0:T(8,128)S(1)} %get-tuple-element.51), channel_id=1, source_target_pairs={{0,4},{8,12},{16,20},{24,28},{4,0},{12,8},{20,16},{28,24},{1,5},{9... | collective-permute-start | bytes 196616 | tf_op jit(solution)/shard_map/ppermute | solution.py:559
  45.2 6.2 %collective-permute-start.3 = (f32[8,2048]{1,0:T(8,128)S(1)}, f32[8,2048]{1,0:T(8,128)S(1)}, u32[]{:S(2)}, u32[]{:S(2)}) collective-permute-start(f32[8,2048]{1,0:T(8,128)S(1)} %get-tuple-element.46), channel_id=1, source_target_pairs={{4,8},{12,16},{20,24},{8,4},{16,12},{24,20},{5,9},{13,17},{21,25},... | collective-permute-start | bytes 196616 | tf_op jit(solution)/shard_map/ppermute | solution.py:559
  46.1 8.1 %collective-permute-start.2 = (f32[8,2048]{1,0:T(8,128)S(1)}, f32[8,2048]{1,0:T(8,128)S(1)}, u32[]{:S(2)}, u32[]{:S(2)}) collective-permute-start(f32[8,2048]{1,0:T(8,128)S(1)} %get-tuple-element.47), channel_id=1, source_target_pairs={{0,4},{8,12},{16,20},{24,28},{4,0},{12,8},{20,16},{28,24},{1,5},{9... | collective-permute-start | bytes 196616 | tf_op jit(solution)/shard_map/ppermute | solution.py:559
  65.2 6.9 %collective-permute-start.5 = (f32[8,2048]{1,0:T(8,128)S(1)}, f32[8,2048]{1,0:T(8,128)S(1)}, u32[]{:S(2)}, u32[]{:S(2)}) collective-permute-start(f32[8,2048]{1,0:T(8,128)S(1)} %get-tuple-element.42), channel_id=1, source_target_pairs={{4,8},{12,16},{20,24},{8,4},{16,12},{24,20},{5,9},{13,17},{21,25},... | collective-permute-start | bytes 196616 | tf_op jit(solution)/shard_map/ppermute | solution.py:559
  65.9 8.5 %collective-permute-start.4 = (f32[8,2048]{1,0:T(8,128)S(1)}, f32[8,2048]{1,0:T(8,128)S(1)}, u32[]{:S(2)}, u32[]{:S(2)}) collective-permute-start(f32[8,2048]{1,0:T(8,128)S(1)} %get-tuple-element.43), channel_id=1, source_target_pairs={{0,4},{8,12},{16,20},{24,28},{4,0},{12,8},{20,16},{28,24},{1,5},{9... | collective-permute-start | bytes 196616 | tf_op jit(solution)/shard_map/ppermute | solution.py:559
  86.1 11.5 %collective-permute-start.7 = (f32[8,1024]{1,0:T(8,128)S(1)}, f32[8,1024]{1,0:T(8,128)S(1)}, u32[]{:S(2)}, u32[]{:S(2)}) collective-permute-start(f32[8,1024]{1,0:T(8,128)S(1)} %get-tuple-element.38), channel_id=1, source_target_pairs={{4,8},{12,16},{20,24},{8,4},{16,12},{24,20},{5,9},{13,17},{21,25},... | collective-permute-start | bytes 98312 | tf_op jit(solution)/shard_map/ppermute | solution.py:559
  86.8 10.8 %collective-permute-start.6 = (f32[8,1024]{1,0:T(8,128)S(1)}, f32[8,1024]{1,0:T(8,128)S(1)}, u32[]{:S(2)}, u32[]{:S(2)}) collective-permute-start(f32[8,1024]{1,0:T(8,128)S(1)} %get-tuple-element.39), channel_id=1, source_target_pairs={{0,4},{8,12},{16,20},{24,28},{4,0},{12,8},{20,16},{28,24},{1,5},{9... | collective-permute-start | bytes 98312 | tf_op jit(solution)/shard_map/ppermute | solution.py:559
  92.5 11.7 %all-to-all-start = ((f32[8,8,128]{2,1,0:T(8,128)}), f32[8,8,128]{2,1,0:T(8,128)S(1)}, u32[]{:S(2)}, u32[]{:S(2)}) async-start(f32[8,8,128]{2,1,0:T(8,128)} %get-tuple-element.34), calls=%async_computation | async-start | bytes 65536 | tf_op jit(solution)/shard_map/all_to_all | solution.py:633
